TPU v7x, 32 devices: a whole 2x2x4 slice. The times are simulated.
32 devices in a mesh: dp: 8 (over z, y), head: 4 (over x, core).
Axes of the slice: x: 2, y: 2, z: 4, core: 2. Of those that a mesh axis runs over, the one named last changes fastest.
Arguments:
- hidden_in: bfloat16 [2048, 2048], P(('dp', 'head')), may hold values from -6 to 6
- norm_gain: bfloat16 [2048], replicated, may hold values from 0.25 to 1.75
- w_query: bfloat16 [2048, 2048], P(None, 'head'), may hold values from -0.125 to 0.125
- key_weight: bfloat16 [2048, 1024], P(None, 'head'), may hold values from -0.125 to 0.125
- w_value: bfloat16 [2048, 1024], P(None, 'head'), may hold values from -0.125 to 0.125
- query_gain: bfloat16 [128], replicated, may hold values from 0.796875 to 4
- key_gain: bfloat16 [128], replicated, may hold values from 0.25 to 1.75
- w_out: bfloat16 [2048, 2048], P('head'), may hold values from -0.125 to 0.125
- prefix_root_keys: bfloat16 [1024, 1024], P('dp', 'head'), may hold values from -210 to 210
- prefix_root_values: bfloat16 [1024, 1024], P('dp', 'head'), may hold values from -6 to 6
- mid_keys: bfloat16 [4096, 1024], P('dp', 'head'), may hold values from -210 to 210
- mid_values: bfloat16 [4096, 1024], P('dp', 'head'), may hold values from -6 to 6
- mid_lengths: int32 [16], replicated, may hold values from 1 to 256, 2048 in all
- leaf_keys: bfloat16 [4096, 1024], P('dp', 'head'), may hold values from -6 to 6
- leaf_values: bfloat16 [4096, 1024], P('dp', 'head'), may hold values from -6 to 6
- leaf_lengths: int32 [64], P('dp'), may hold values from 1 to 64, 2048 in all
- token_request: int32 [8, 256], P('dp'), may hold values from 0 to 7, never falling along the last dimension, each value on 1 to 64 neighbouring positions
- request_node: int32 [8, 8], P('dp'), may hold values from 0 to 15, as said below
Outputs:
- attn_update: bfloat16 [2048, 2048], P(('dp', 'head'))
- cache_keys: bfloat16 [2048, 1024], P('dp', 'head')
- cache_values: bfloat16 [2048, 1024], P('dp', 'head')
Inputs may be any that keep to these rules, and one draw needn't show every extreme that they name: `token_request`: in each row requests 0 to 7 all occur, in rising order, each on 1 to 64 consecutive tokens; some request has exactly 64. `request_node`: node v is held by dp index v // 2; the 8 requests of one row have parents on 8 different dp indices, one each.
All inputs are finite; a program needn't handle non-finite values. No bound on the sum of `leaf_lengths` on one device may be relied on, other than what follows from the above.
Results may differ from a plain program's by a relative error of at most 0.039.
Values may be sent and summed in bfloat16 or wider, within the bound.
A program may use at most 128 MiB of HBM per device.

v0:
```python
import math
import jax
import jax.numpy as jnp
from jax import lax
from jax.sharding import PartitionSpec as P

MID_DEV = 2
MID_LEN = 256
EPS = 1e-06
THETA = 1000000.0
MASKED = -1e30


def rms_rows(values, gain):
    power = jnp.mean(values * values, axis=-1, keepdims=True)
    return values * lax.rsqrt(power + EPS) * gain


def rotate(values, positions):
    width = values.shape[-1]
    half = width // 2
    exponent = jnp.arange(half).astype(jnp.float32) * (2.0 / width)
    freqs = jnp.power(THETA, -exponent)
    angles = positions.astype(jnp.float32)[:, None] * freqs[None, :]
    cosine = jnp.cos(angles)[:, None, :]
    sine = jnp.sin(angles)[:, None, :]
    first = values[..., :half]
    second = values[..., half:]
    return jnp.concatenate(
        [first * cosine - second * sine, second * cosine + first * sine], axis=-1
    )


def body(
    hidden_in,
    norm_gain,
    w_query,
    key_weight,
    w_value,
    query_gain,
    key_gain,
    w_out,
    prefix_root_keys,
    prefix_root_values,
    mid_keys,
    mid_values,
    mid_lengths,
    leaf_keys,
    leaf_values,
    leaf_lengths,
    token_request,
    request_node,
):
    head_dim = query_gain.shape[0]
    query_width = w_query.shape[1]
    key_width = key_weight.shape[1]
    kv_heads = key_width // head_dim
    query_group = query_width // key_width
    scale = 1.0 / math.sqrt(head_dim)
    dp_count = lax.axis_size("dp")
    normalized_input = rms_rows(
        hidden_in.astype(jnp.float32), norm_gain.astype(jnp.float32)
    ).astype(jnp.bfloat16)
    piece = lax.all_gather(normalized_input, "head", axis=0, tiled=True)
    mixed = jnp.concatenate(
        [
            jnp.dot(piece, w_query, preferred_element_type=jnp.float32),
            jnp.dot(piece, key_weight, preferred_element_type=jnp.float32),
            jnp.dot(piece, w_value, preferred_element_type=jnp.float32),
        ],
        axis=1,
    )
    height = mixed.shape[0]
    segment = token_request[0]
    branch_nodes = request_node[0]
    requests = branch_nodes.shape[0]
    request_ids = jnp.arange(requests, dtype=jnp.int32)
    token_ids = jnp.arange(height, dtype=jnp.int32)
    member = segment[None, :] == request_ids[:, None]
    counts = jnp.sum(member.astype(jnp.int32), axis=1)
    earlier = request_ids[None, :] < request_ids[:, None]
    starts = jnp.sum(jnp.where(earlier, counts[None, :], 0), axis=1)
    offset = token_ids - jnp.sum(jnp.where(member, starts[:, None], 0), axis=0)
    node_total = mid_lengths.shape[0]
    node_match = branch_nodes[:, None] == jnp.arange(node_total, dtype=jnp.int32)[None, :]
    branch_length = jnp.sum(jnp.where(node_match, mid_lengths[None, :], 0), axis=1)
    root_total = prefix_root_keys.shape[0] * dp_count
    positions = (
        root_total
        + jnp.sum(jnp.where(member, (branch_length + leaf_lengths)[:, None], 0), axis=0)
        + offset
    )
    query_part = mixed[:, :query_width].reshape(height, query_width // head_dim, head_dim)
    key_portion = mixed[:, query_width : query_width + key_width].reshape(
        height, kv_heads, head_dim
    )
    query_matrix = rotate(rms_rows(query_part, query_gain.astype(jnp.float32)), positions).astype(
        jnp.bfloat16
    )
    new_keys = rotate(rms_rows(key_portion, key_gain.astype(jnp.float32)), positions).astype(
        jnp.bfloat16
    )
    new_values = mixed[:, query_width + key_width :].astype(jnp.bfloat16)
    heads_query = query_matrix.reshape(height, kv_heads, query_group, head_dim)
    root_keys = lax.all_gather(prefix_root_keys, "dp", axis=0, tiled=True)
    root_values = lax.all_gather(prefix_root_values, "dp", axis=0, tiled=True)
    owner_of = branch_nodes // MID_DEV
    owner_ids = jnp.arange(dp_count, dtype=jnp.int32)
    owner_match = owner_of[None, :] == owner_ids[:, None]
    block_slot = jnp.sum(jnp.where(owner_match, (branch_nodes % MID_DEV)[None, :], 0), axis=1)
    block_request = jnp.sum(jnp.where(owner_match, request_ids[None, :], 0), axis=1)
    block_length = jnp.sum(jnp.where(owner_match, branch_length[None, :], 0), axis=1)
    wanted = lax.all_to_all(block_slot[:, None], "dp", split_axis=0, concat_axis=0, tiled=True)[
        :, 0
    ]
    second = (wanted == 1)[:, None, None]
    own_pairs = jnp.concatenate([mid_keys, mid_values], axis=1).reshape(
        MID_DEV, MID_LEN, 2 * key_width
    )
    sent = jnp.where(second, own_pairs[1][None], own_pairs[0][None])
    got = lax.all_to_all(sent, "dp", split_axis=0, concat_axis=0, tiled=True)
    got = got.reshape(dp_count * MID_LEN, 2 * key_width)
    leaf_each = leaf_keys.shape[0] // requests
    leaf_live = jnp.arange(leaf_each, dtype=jnp.int32)[None, :] < leaf_lengths[:, None]
    leaf_tag = jnp.where(leaf_live, request_ids[:, None], -1).reshape(-1)
    mid_live = jnp.arange(MID_LEN, dtype=jnp.int32)[None, :] < block_length[:, None]
    mid_tag = jnp.where(mid_live, block_request[:, None], -1).reshape(-1)
    own_mask = (segment[None, :] == segment[:, None]) & (token_ids[None, :] <= token_ids[:, None])
    mask = jnp.concatenate(
        [
            jnp.ones((height, root_keys.shape[0]), jnp.bool_),
            leaf_tag[None, :] == segment[:, None],
            own_mask,
            mid_tag[None, :] == segment[:, None],
        ],
        axis=1,
    )
    all_keys = jnp.concatenate(
        [root_keys, leaf_keys, new_keys.reshape(height, key_width), got[:, :key_width]], axis=0
    ).reshape(-1, kv_heads, head_dim)
    all_values = jnp.concatenate(
        [root_values, leaf_values, new_values, got[:, key_width:]], axis=0
    ).reshape(-1, kv_heads, head_dim)
    scores = jnp.einsum("tkgd,skd->kgts", heads_query, all_keys, preferred_element_type=jnp.float32)
    scores = jnp.where(mask[None, None], scores * scale, MASKED)
    weights = jnp.exp(scores - jnp.max(scores, axis=-1, keepdims=True))
    total = jnp.sum(weights, axis=-1)
    summed = jnp.einsum(
        "kgts,skd->kgtd",
        weights.astype(jnp.bfloat16),
        all_values,
        preferred_element_type=jnp.float32,
    )
    attn = (summed / total[..., None]).astype(jnp.bfloat16)
    attn = attn.transpose(2, 0, 1, 3).reshape(height, query_width)
    update = lax.psum_scatter(
        jnp.dot(attn, w_out, preferred_element_type=jnp.float32).astype(jnp.bfloat16),
        "head",
        scatter_dimension=0,
        tiled=True,
    )
    return (update, new_keys.reshape(height, key_width), new_values)


def solution(mesh):
    in_specs = (
        P(("dp", "head"), None),
        P(),
        P(None, "head"),
        P(None, "head"),
        P(None, "head"),
        P(),
        P(),
        P("head", None),
        P("dp", "head"),
        P("dp", "head"),
        P("dp", "head"),
        P("dp", "head"),
        P(),
        P("dp", "head"),
        P("dp", "head"),
        P("dp"),
        P("dp", None),
        P("dp", None),
    )
    out_specs = (P(("dp", "head"), None), P("dp", "head"), P("dp", "head"))
    return jax.shard_map(body, mesh=mesh, in_specs=in_specs, out_specs=out_specs, check_vma=False)
```

profile of v0, /device:TPU:0, one launch (start us, length us, event | category | flops | bytes accessed | tf_op | source)
XLA Modules:
  0.0 206.7 jit_solution(16049318135466380190)
XLA Ops:
  9.7 7.3 %all-to-all-start = ((s32[8,1,1]{2,1,0:T(1,128)}), s32[8,1,1]{2,1,0:T(1,128)S(1)}, u32[]{:S(2)}, u32[]{:S(2)}) async-start(s32[8,1,1]{2,1,0:T(1,128)} %copy.122), calls=%async_computation | async-start | bytes 8192 | tf_op jit(solution)/shard_map/all_to_all | solution.py:113
  18.8 1.8 fusion.24
  25.8 29.8 %all_gather.11 = bf16[1024,256]{0,1:T(8,128)(2,1)} all-gather(bf16[128,256]{0,1:T(8,128)(2,1)S(1)} %copy.133), channel_id=1, replica_groups=mesh['dp'=8,'head'=4] {'dp'}, dimensions={0}, use_global_device_ids=true | all-gather | bytes 589824 | tf_op jit(solution)/shard_map/all_gather | solution.py:106
  56.5 27.1 %all_gather.9 = bf16[1024,256]{0,1:T(8,128)(2,1)S(1)} all-gather(bf16[128,256]{0,1:T(8,128)(2,1)S(1)} %copy.119), channel_id=1, replica_groups=mesh['dp'=8,'head'=4] {'dp'}, dimensions={0}, use_global_device_ids=true | all-gather | bytes 589824 | tf_op jit(solution)/shard_map/all_gather | solution.py:105
  84.4 1.8 copy.124
  86.2 1.8 copy.123
  88.0 1.8 copy.134
  91.1 1.8 copy.120
  92.9 1.8 copy.127
  96.0 2.7 %broadcast_select_fusion = bf16[8,256,512]{1,2,0:T(8,128)(2,1)} fusion(pred[8]{0:T(512)(128)(4,1)S(1)} %compare_reduce_fusion, bf16[256,512]{0,1:T(8,128)(2,1)} %copy.124, bf16[256,512]{0,1:T(8,128)(2,1)} %copy.123), kind=kLoop, calls=%fused_computation.9 | loop fusion | flops 1048576 | bytes 2621448 | tf_op jit(solution)/shard_map/jit(_where)/select_n | solution.py:120
  98.6 4.4 %all-to-all-start.1 = ((bf16[8,256,512]{1,2,0:T(8,128)(2,1)}), bf16[8,256,512]{1,2,0:T(8,128)(2,1)}, u32[]{:S(2)}, u32[]{:S(2)}) async-start(bf16[8,256,512]{1,2,0:T(8,128)(2,1)} %broadcast_select_fusion), calls=%async_computation.1 | async-start | bytes 4194304 | tf_op jit(solution)/shard_map/all_to_all | solution.py:121
  103.2 7.0 %pad_add_fusion = pred[256,3840]{0,1:T(8,128)(4,1)} fusion(pred[256,2048]{0,1:T(8,128)(4,1)S(1)} %broadcast_compare_fusion, pred[256,256]{0,1:T(8,128)(4,1)S(1)} %fusion.28, pred[256,512]{0,1:T(8,128)(4,1)S(1)} %broadcast_compare_fusion.1, pred[3840]{0:T(1024)(128)(4,1)S(1)} %pad.8.clone), kind=kLoop, calls=%fused_computation.7 | loop fusion | flops 2949120 | bytes 1707776 | tf_op jit(solution)/shard_map/concatenate | solution.py:129
  110.2 2.0 convolution_convert_fusion.1
  112.9 2.6 %fusion.36 = f32[256,512]{1,0:T(8,128)S(1)} fusion(bf16[256,2048]{1,0:T(8,128)(2,1)} %all-gather.2.cloned.1.call-done, bf16[2048,512]{1,0:T(8,128)(2,1)} %param.20), kind=kOutput, calls=%fused_computation.82 | convolution fusion | flops 536870912 | bytes 3670016 | tf_op jit(solution)/shard_map/dot_general | solution.py:67
  119.6 22.3 %all-to-all-done.1 = bf16[8,256,512]{1,2,0:T(8,128)(2,1)} async-done(((bf16[8,256,512]{1,2,0:T(8,128)(2,1)}), bf16[8,256,512]{1,2,0:T(8,128)(2,1)}, u32[]{:S(2)}, u32[]{:S(2)}) %all-to-all-start.1) | async-done | bytes 2097184 | tf_op jit(solution)/shard_map/all_to_all | solution.py:121
  141.9 1.9 copy.142
  143.8 1.1 fusion.34
  145.0 1.3 copy.128
  146.3 10.1 %fusion.2 = (f32[2,2,256]{2,1,0:T(2,128)S(1)}, f32[2,3840,256,2]{2,1,3,0:T(8,128)}) fusion(pred[256,3840]{0,1:T(8,128)(4,1)} %pad_add_fusion, bf16[256,2,2,64]{3,0,2,1:T(8,128)(2,1)} %bitcast.71, bf16[256,2,2,64]{3,0,2,1:T(8,128)(2,1)} %bitcast.72, bf16[2048,2,128]{2,0,1:T(8,128)(2,1)} %copy.128, bf16[256,2,128]{2,0,1:T(8,128)(2,1)S(1)} %maximum_convert_fusion, ...), kind=kOutput, calls=%fused_computation.4 | convolution fusion | flops 1026817024 | bytes 18944000 | tf_op jit(solution)/shard_map/tkgd,skd->kgts/dot_general | solution.py:144
  156.4 9.1 %fusion = f32[2,2,256]{2,1,0:T(2,128)S(1)} fusion(f32[2,3840,256,2]{2,1,3,0:T(8,128)} %get-tuple-element.41, f32[2,2,256]{2,1,0:T(2,128)S(1)} %get-tuple-element.40, pred[256,3840]{0,1:T(8,128)(4,1)} %pad_add_fusion), kind=kLoop, calls=%fused_computation.2 | loop fusion | flops 15727616 | bytes 16719872 | tf_op jit(solution)/shard_map/reduce_sum | solution.py:147
  165.5 1.2 pad_maximum_fusion
  166.8 7.7 %fusion.19 = bf16[256,2,2,128]{0,3,2,1:T(8,128)(2,1)S(1)} fusion(bf16[3840,2,128,1]{0,2,3,1:T(8,128)(2,1)S(1)} %bitcast.67, f32[2,3840,256,2]{2,1,3,0:T(8,128)} %get-tuple-element.41, f32[2,2,256]{2,1,0:T(2,128)S(1)} %get-tuple-element.40, pred[256,3840]{0,1:T(8,128)(4,1)S(1)} %copy-done.3, f32[256,2,2]{0,2,1:T(2,128)S(1)} %bitcast.80), kind=kOutput, calls=%fused_computation.22 | convolution fusion | flops 1022623744 | bytes 18948096 | tf_op jit(solution)/shard_map/kgts,skd->kgtd/dot_general | solution.py:148
  174.5 1.7 convolution_convert_fusion
  177.2 22.7 %reduce-scatter.2.cloned.1.call-done = bf16[64,2048]{1,0:T(8,128)(2,1)} async-done(((bf16[256,2048]{1,0:T(8,128)(2,1)}), bf16[64,2048]{1,0:T(8,128)(2,1)}) %reduce-scatter.2.cloned.1.call-update) | async-done | bytes 262160 | tf_op jit(solution)/shard_map/reduce_scatter | solution.py:156
  (80 shorter events, 19.7 us)
Async XLA Ops:
  7.2 167.4 %copy-start = (bf16[512,2048]{1,0:T(8,128)(2,1)S(1)}, bf16[512,2048]{1,0:T(8,128)(2,1)}, u32[]{:S(2)}) copy-start(bf16[512,2048]{1,0:T(8,128)(2,1)} %param.25) | copy-start | bytes 6291460
  7.2 48.5 %copy-start.12 = (s32[1,256]{1,0:T(1,128)S(1)}, s32[1,256]{1,0:T(1,128)}, u32[]{:S(2)}) copy-start(s32[1,256]{1,0:T(1,128)} %param.34) | copy-start | bytes 3076
  7.2 49.2 %copy-start.11 = (bf16[128,256]{1,0:T(8,128)(2,1)S(1)}, bf16[128,256]{1,0:T(8,128)(2,1)}, u32[]{:S(2)}) copy-start(bf16[128,256]{1,0:T(8,128)(2,1)} %param.26) | copy-start | bytes 196612
  9.7 86.0 %all-to-all-start = ((s32[8,1,1]{2,1,0:T(1,128)}), s32[8,1,1]{2,1,0:T(1,128)S(1)}, u32[]{:S(2)}, u32[]{:S(2)}) async-start(s32[8,1,1]{2,1,0:T(1,128)} %copy.122), calls=%async_computation | async-start | bytes 8192 | tf_op jit(solution)/shard_map/all_to_all | solution.py:113
  17.0 93.2 %all-gather.2.cloned.1.call-start = ((), (), s32[]{:S(2)}) async-start(), calls=%async_computation.3 | async-start | bytes 1310720 | tf_op jit(solution)/shard_map/all_gather | solution.py:64
  98.6 43.3 %all-to-all-start.1 = ((bf16[8,256,512]{1,2,0:T(8,128)(2,1)}), bf16[8,256,512]{1,2,0:T(8,128)(2,1)}, u32[]{:S(2)}, u32[]{:S(2)}) async-start(bf16[8,256,512]{1,2,0:T(8,128)(2,1)} %broadcast_select_fusion), calls=%async_computation.1 | async-start | bytes 4194304 | tf_op jit(solution)/shard_map/all_to_all | solution.py:121
  103.0 96.9 %reduce-scatter.2.cloned.1.call-start = ((), (), s32[]{:S(2)}) async-start(), calls=%async_computation.4 | async-start | bytes 1310720 | tf_op jit(solution)/shard_map/reduce_scatter | solution.py:156
  112.1 4.9 %copy-start.6 = (bf16[256,256]{1,0:T(8,128)(2,1)}, bf16[256,256]{1,0:T(8,128)(2,1)S(1)}, u32[]{:S(2)}) copy-start(bf16[256,256]{1,0:T(8,128)(2,1)S(1)} %convolution_convert_fusion.1) | copy-start | bytes 393220
  115.7 2.8 %copy-start.1 = (bf16[256,2048]{1,0:T(8,128)(2,1)S(1)}, bf16[256,2048]{1,0:T(8,128)(2,1)}, u32[]{:S(2)}) copy-start(bf16[256,2048]{1,0:T(8,128)(2,1)} %all-gather.2.cloned.1.call-done) | copy-start | bytes 3145732
  115.7 2.8 %copy-start.4 = (bf16[2048,256]{1,0:T(8,128)(2,1)S(1)}, bf16[2048,256]{1,0:T(8,128)(2,1)}, u32[]{:S(2)}) copy-start(bf16[2048,256]{1,0:T(8,128)(2,1)} %param.21) | copy-start | bytes 3145732
  119.6 26.7 %copy-start.8 = (bf16[256,2,128]{2,0,1:T(8,128)(2,1)}, bf16[256,2,128]{2,0,1:T(8,128)(2,1)S(1)}, u32[]{:S(2)}) copy-start(bf16[256,2,128]{2,0,1:T(8,128)(2,1)S(1)} %maximum_convert_fusion) | copy-start | bytes 393220
  143.8 2.5 %copy-start.10 = (bf16[512,2,128]{2,0,1:T(8,128)(2,1)S(1)}, bf16[512,2,128]{2,0,1:T(8,128)(2,1)}, u32[]{:S(2)}) copy-start(bf16[512,2,128]{2,0,1:T(8,128)(2,1)} %copy.127) | copy-start | bytes 786436
  156.3 9.1 %copy-start.2 = (bf16[2048,256]{0,1:T(8,128)(2,1)S(1)}, bf16[2048,256]{0,1:T(8,128)(2,1)}, u32[]{:S(2)}) copy-start(bf16[2048,256]{0,1:T(8,128)(2,1)} %get-tuple-element.27) | copy-start | bytes 3145732
  156.3 9.1 %copy-start.5 = (bf16[512,256]{0,1:T(8,128)(2,1)S(1)}, bf16[512,256]{0,1:T(8,128)(2,1)}, u32[]{:S(2)}) copy-start(bf16[512,256]{0,1:T(8,128)(2,1)} %copy.134) | copy-start | bytes 786436
  156.3 9.1 %copy-start.7 = (bf16[256,256]{0,1:T(8,128)(2,1)S(1)}, bf16[256,256]{0,1:T(8,128)(2,1)}, u32[]{:S(2)}) copy-start(bf16[256,256]{0,1:T(8,128)(2,1)} %copy.135) | copy-start | bytes 393220
  165.4 1.4 copy-start.3
  174.5 1.8 copy-start.9
Sparse Core Ops, SparseCore 0:
  20.8 18.0 all-gather.1
  176.4 23.4 reduce-scatter.1
where the time goes:
time: 208 us; the launch traced here: 207 us
  blocking collectives  56.8 us (27%)
  waiting for transfers between devices  45.1 us (22%)
  other arithmetic  31.6 us (15%)
  matrix products  24.6 us (12%)
  local copies, waits for them, and re-layouts  22.5 us (11%)
  between operations  14.4 us (7%)
  starting transfers between devices  11.7 us (6%)
    all_gather x1, blocking collectives, body(): root_values = lax.all_gather(prefix_root_values, 'dp', axis=0, tiled=True)  29.8 us
    all_gather x1, blocking collectives, body(): root_keys = lax.all_gather(prefix_root_keys, 'dp', axis=0, tiled=True)  27.1 us
    reduce_scatter x1, waiting for transfers between devices, body(): lax.psum_scatter(jnp.dot(attn, w_out, preferred_element_type=jnp.float32)...  22.7 us
    all_to_all x1, waiting for transfers between devices, body(): got = lax.all_to_all(sent, 'dp', split_axis=0, concat_axis=0, tiled=True)  22.3 us
    dot_general x1, matrix products, body(): jnp.einsum('tkgd,skd->kgts', heads_query, all_keys, preferred_element_typ...  10.1 us
    reduce_sum x1, other arithmetic, body(): total = jnp.sum(weights, axis=-1)  9.09 us
    dot_general x1, matrix products, body(): jnp.einsum('kgts,skd->kgtd', weights.astype(jnp.bfloat16), all_values, pr...  7.7 us
    all_to_all x1, starting transfers between devices, body(): lax.all_to_all(block_slot[:, None], 'dp', split_axis=0, concat_axis=0, ti...  7.28 us
  transfers between devices with their start and end apart: 4, of which 2 were waited for; matrix products, arithmetic and copies ran while one was open for 20% of the time, Pallas kernels for 0%

commit v1 on v0

--- a/solution.py
+++ b/solution.py
@@ -102,8 +102,10 @@
     )
     new_values = mixed[:, query_width + key_width :].astype(jnp.bfloat16)
     heads_query = query_matrix.reshape(height, kv_heads, query_group, head_dim)
-    root_keys = lax.all_gather(prefix_root_keys, "dp", axis=0, tiled=True)
-    root_values = lax.all_gather(prefix_root_values, "dp", axis=0, tiled=True)
+    z1 = lax.all_gather(
+        jnp.concatenate([prefix_root_keys, prefix_root_values], 1), "dp", axis=0, tiled=True
+    )
+    root_keys, root_values = jnp.split(z1, [prefix_root_keys.shape[1]], 1)
     owner_of = branch_nodes // MID_DEV
     owner_ids = jnp.arange(dp_count, dtype=jnp.int32)
     owner_match = owner_of[None, :] == owner_ids[:, None]

time: 208 us -> 171 us (0.82)
  blocking collectives: 56.8 us -> 0 us
  waiting for transfers between devices: 45.1 us -> 63.2 us
  other arithmetic: 31.6 us -> 36.6 us
  local copies, waits for them, and re-layouts: 22.5 us -> 18.6 us
    all_gather x2 -> x0, blocking collectives: 56.8 us -> none  [the longest x1 29.8 us: body(): root_values = lax.all_gather(prefix_root_values, 'dp', axis=0, tiled=True)]
    all_gather x0 -> x1, waiting for transfers between devices: none -> 36.3 us  [body(): lax.all_gather(jnp.concatenate([prefix_root_keys, prefix_root_values], 1)...]
    all_to_all x1, waiting for transfers between devices: 22.3 us -> 2.8 us  [body(): got = lax.all_to_all(sent, 'dp', split_axis=0, concat_axis=0, tiled=True)]
    slice x3, local copies, waits for them, and re-layouts: 4.43 us -> 0.3 us  [body(): sent = jnp.where(second, own_pairs[1][None], own_pairs[0][None])]
    unnamed x33 -> x37, local copies, waits for them, and re-layouts: 6.52 us -> 5.72 us
  transfers between devices with their start and end apart: 4 -> 5, of which waited for: 2 -> 3; matrix products, arithmetic and copies ran while one was open for 20% -> 25% of each run, Pallas kernels for 0% -> 0%
where the time goes in v1:
time: 171 us
  waiting for transfers between devices  63.2 us (37%)
  other arithmetic  36.6 us (21%)
  matrix products  24.6 us (14%)
  local copies, waits for them, and re-layouts  18.6 us (11%)
  between operations  14.1 us (8%)
  starting transfers between devices  13.5 us (8%)
    all_gather x1, waiting for transfers between devices, body(): lax.all_gather(jnp.concatenate([prefix_root_keys, prefix_root_values], 1)...  36.3 us
    reduce_scatter x1, waiting for transfers between devices, body(): lax.psum_scatter(jnp.dot(attn, w_out, preferred_element_type=jnp.float32)...  24 us
    dot_general x1, matrix products, body(): jnp.einsum('tkgd,skd->kgts', heads_query, all_keys, preferred_element_typ...  10.1 us
    reduce_sum x1, other arithmetic, body(): total = jnp.sum(weights, axis=-1)  9.09 us
    dot_general x1, matrix products, body(): jnp.einsum('kgts,skd->kgtd', weights.astype(jnp.bfloat16), all_values, pr...  7.7 us
    all_to_all x1, starting transfers between devices, body(): lax.all_to_all(block_slot[:, None], 'dp', split_axis=0, concat_axis=0, ti...  7.28 us
    concatenate x1, other arithmetic, body(): jnp.concatenate([jnp.ones((height, root_keys.shape[0]), jnp.bool_), leaf_...  6.99 us
    all_to_all x1, starting transfers between devices, body(): got = lax.all_to_all(sent, 'dp', split_axis=0, concat_axis=0, tiled=True)  6.11 us
  transfers between devices with their start and end apart: 5, of which 3 were waited for; matrix products, arithmetic and copies ran while one was open for 25% of the time, Pallas kernels for 0%

profile of v1, /device:TPU:0, one launch (start us, length us, event | category | flops | bytes accessed | tf_op | source)
XLA Modules:
  0.0 170.7 jit_solution(8407628438155703135)
XLA Ops:
  9.2 1.8 %fusion.24 = bf16[64,2048]{1,0:T(8,128)(2,1)} fusion(bf16[64,2048]{1,0:T(8,128)(2,1)} %param.18, f32[2048]{0:T(1024)S(1)} %convert_element_type.58, f32[64]{0:T(128)S(1)} %add_rsqrt_fusion.2), kind=kLoop, calls=%fused_computation.28 | loop fusion | flops 524288 | bytes 532736 | tf_op jit(solution)/shard_map/convert_element_type | solution.py:63
  13.4 7.3 %all-to-all-start = ((s32[8,1,1]{2,1,0:T(1,128)}), s32[8,1,1]{2,1,0:T(1,128)S(1)}, u32[]{:S(2)}, u32[]{:S(2)}) async-start(s32[8,1,1]{2,1,0:T(1,128)} %copy.123), calls=%async_computation | async-start | bytes 8192 | tf_op jit(solution)/shard_map/all_to_all | solution.py:115
  24.6 1.2 add.74
  25.8 1.5 fusion.28
  27.3 1.3 convert_reduce_fusion
  32.5 1.3 select_reduce_fusion.3
  37.2 1.1 multiply_cosine_fusion
  38.6 1.6 broadcast_select_fusion
  40.1 6.1 %all-to-all-start.1 = ((bf16[8,256,512]{1,2,0:T(8,128)(2,1)}), bf16[8,256,512]{1,2,0:T(8,128)(2,1)}, u32[]{:S(2)}, u32[]{:S(2)}) async-start(bf16[8,256,512]{1,2,0:T(8,128)(2,1)} %broadcast_select_fusion), calls=%async_computation.1 | async-start | bytes 4194304 | tf_op jit(solution)/shard_map/all_to_all | solution.py:123
  46.3 7.0 %pad_add_fusion = pred[256,3840]{0,1:T(8,128)(4,1)} fusion(pred[256,2048]{0,1:T(8,128)(4,1)S(1)} %broadcast_compare_fusion, pred[256,256]{0,1:T(8,128)(4,1)S(1)} %copy-done.12, pred[256,512]{0,1:T(8,128)(4,1)S(1)} %broadcast_compare_fusion.1, pred[3840]{0:T(1024)(128)(4,1)S(1)} %pad.8.clone), kind=kLoop, calls=%fused_computation.7 | loop fusion | flops 2949120 | bytes 1707776 | tf_op jit(solution)/shard_map/concatenate | solution.py:131
  53.3 2.0 %convolution_convert_fusion.1 = bf16[256,256]{1,0:T(8,128)(2,1)S(1)} fusion(bf16[256,2048]{1,0:T(8,128)(2,1)} %all-gather.5.cloned.1.call-done, bf16[2048,256]{1,0:T(8,128)(2,1)} %param.22), kind=kOutput, calls=%fused_computation.20 | convolution fusion | flops 268500992 | bytes 2228224 | tf_op jit(solution)/shard_map/dot_general | solution.py:69
  56.1 2.6 %fusion.37 = f32[256,512]{1,0:T(8,128)S(1)} fusion(bf16[256,2048]{1,0:T(8,128)(2,1)} %all-gather.5.cloned.1.call-done, bf16[2048,512]{1,0:T(8,128)(2,1)} %param.20), kind=kOutput, calls=%fused_computation.84 | convolution fusion | flops 536870912 | bytes 3670016 | tf_op jit(solution)/shard_map/dot_general | solution.py:67
  62.8 36.3 %all-gather.3.cloned.1.call-done = bf16[1024,512]{0,1:T(8,128)(2,1)} async-done(((bf16[128,512]{0,1:T(8,128)(2,1)}), bf16[1024,512]{0,1:T(8,128)(2,1)}) %all-gather.3.cloned.1.call-update) | async-done | bytes 1048592 | tf_op jit(solution)/shard_map/all_gather | solution.py:105
  99.1 2.1 %fusion.35 = (bf16[1024,256]{0,1:T(8,128)(2,1)S(1)}, bf16[1024,256]{0,1:T(8,128)(2,1)}) fusion(bf16[1024,512]{0,1:T(8,128)(2,1)} %all-gather.3.cloned.1.call-done), kind=kLoop, calls=%fused_computation.82 | loop fusion | bytes 2097152 | tf_op jit(solution)/shard_map/split | solution.py:108
  102.1 2.8 %all-to-all-done.1 = bf16[8,256,512]{1,2,0:T(8,128)(2,1)} async-done(((bf16[8,256,512]{1,2,0:T(8,128)(2,1)}), bf16[8,256,512]{1,2,0:T(8,128)(2,1)}, u32[]{:S(2)}, u32[]{:S(2)}) %all-to-all-start.1) | async-done | bytes 2097184 | tf_op jit(solution)/shard_map/all_to_all | solution.py:123
  104.9 1.9 %copy.142 = bf16[8,64,8,256]{3,2,0,1:T(8,128)(2,1)S(1)} copy(bf16[8,64,8,256]{3,2,1,0:T(8,128)(2,1)} %bitcast.24) | data formatting | bytes 4194304 | tf_op jit(solution)/shard_map/reshape | solution.py:124
  106.8 1.1 fusion.34
  107.9 1.3 copy.129
  109.3 10.1 %fusion.2 = (f32[2,2,256]{2,1,0:T(2,128)S(1)}, f32[2,3840,256,2]{2,1,3,0:T(8,128)}) fusion(pred[256,3840]{0,1:T(8,128)(4,1)} %pad_add_fusion, bf16[256,2,2,64]{3,0,2,1:T(8,128)(2,1)} %bitcast.71, bf16[256,2,2,64]{3,0,2,1:T(8,128)(2,1)} %bitcast.72, bf16[2048,2,128]{2,0,1:T(8,128)(2,1)} %copy.129, bf16[256,2,128]{2,0,1:T(8,128)(2,1)S(1)} %maximum_convert_fusion, ...), kind=kOutput, calls=%fused_computation.4 | convolution fusion | flops 1026817024 | bytes 18944000 | tf_op jit(solution)/shard_map/tkgd,skd->kgts/dot_general | solution.py:146
  119.3 9.1 %fusion = f32[2,2,256]{2,1,0:T(2,128)S(1)} fusion(f32[2,3840,256,2]{2,1,3,0:T(8,128)} %get-tuple-element.43, f32[2,2,256]{2,1,0:T(2,128)S(1)} %get-tuple-element.42, pred[256,3840]{0,1:T(8,128)(4,1)} %pad_add_fusion), kind=kLoop, calls=%fused_computation.2 | loop fusion | flops 15727616 | bytes 16719872 | tf_op jit(solution)/shard_map/reduce_sum | solution.py:149
  128.5 1.2 pad_maximum_fusion
  129.8 7.7 %fusion.19 = bf16[256,2,2,128]{0,3,2,1:T(8,128)(2,1)S(1)} fusion(bf16[3840,2,128,1]{0,2,3,1:T(8,128)(2,1)S(1)} %bitcast.67, f32[2,3840,256,2]{2,1,3,0:T(8,128)} %get-tuple-element.43, f32[2,2,256]{2,1,0:T(2,128)S(1)} %get-tuple-element.42, pred[256,3840]{0,1:T(8,128)(4,1)S(1)} %copy-done.3, f32[256,2,2]{0,2,1:T(2,128)S(1)} %bitcast.80), kind=kOutput, calls=%fused_computation.22 | convolution fusion | flops 1022623744 | bytes 18948096 | tf_op jit(solution)/shard_map/kgts,skd->kgtd/dot_general | solution.py:150
  137.5 1.7 %convolution_convert_fusion = bf16[256,2048]{1,0:T(8,128)(2,1)} fusion(bf16[256,512]{0,1:T(8,128)(2,1)S(1)} %bitcast.73, bf16[512,2048]{1,0:T(8,128)(2,1)S(1)} %copy-done), kind=kOutput, calls=%fused_computation.8 | convolution fusion | flops 537395200 | bytes 3407872 | tf_op jit(solution)/shard_map/dot_general | solution.py:159
  140.1 24.0 %reduce-scatter.2.cloned.1.call-done = bf16[64,2048]{1,0:T(8,128)(2,1)} async-done(((bf16[256,2048]{1,0:T(8,128)(2,1)}), bf16[64,2048]{1,0:T(8,128)(2,1)}) %reduce-scatter.2.cloned.1.call-update) | async-done | bytes 262160 | tf_op jit(solution)/shard_map/reduce_scatter | solution.py:158
  (87 shorter events, 22.5 us)
Async XLA Ops:
  7.2 130.3 %copy-start = (bf16[512,2048]{1,0:T(8,128)(2,1)S(1)}, bf16[512,2048]{1,0:T(8,128)(2,1)}, u32[]{:S(2)}) copy-start(bf16[512,2048]{1,0:T(8,128)(2,1)} %param.25) | copy-start | bytes 6291460
  7.2 24.6 %copy-start.13 = (s32[1,256]{1,0:T(1,128)S(1)}, s32[1,256]{1,0:T(1,128)}, u32[]{:S(2)}) copy-start(s32[1,256]{1,0:T(1,128)} %param.34) | copy-start | bytes 3076
  7.2 23.6 %copy-start.10 = (bf16[512,256]{1,0:T(8,128)(2,1)S(1)}, bf16[512,256]{1,0:T(8,128)(2,1)}, u32[]{:S(2)}) copy-start(bf16[512,256]{1,0:T(8,128)(2,1)} %param.32) | copy-start | bytes 786436
  7.2 25.3 %copy-start.14 = (bf16[128]{0:T(256)(128)(2,1)S(1)}, bf16[128]{0:T(256)(128)(2,1)}, u32[]{:S(2)}) copy-start(bf16[128]{0:T(256)(128)(2,1)} %param.23) | copy-start | bytes 772
  7.2 46.1 %all-gather.5.cloned.1.call-start = ((), (), s32[]{:S(2)}) async-start(), calls=%async_computation.4 | async-start | bytes 1310720 | tf_op jit(solution)/shard_map/all_gather | solution.py:64
  13.4 24.9 %all-to-all-start = ((s32[8,1,1]{2,1,0:T(1,128)}), s32[8,1,1]{2,1,0:T(1,128)S(1)}, u32[]{:S(2)}, u32[]{:S(2)}) async-start(s32[8,1,1]{2,1,0:T(1,128)} %copy.123), calls=%async_computation | async-start | bytes 8192 | tf_op jit(solution)/shard_map/all_to_all | solution.py:115
  20.7 78.4 %all-gather.3.cloned.1.call-start = ((), (), s32[]{:S(2)}) async-start(), calls=%async_computation.3 | async-start | bytes 1179648 | tf_op jit(solution)/shard_map/all_gather | solution.py:105
  40.1 6.2 %copy-start.12 = (pred[256,256]{0,1:T(8,128)(4,1)S(1)}, pred[256,256]{0,1:T(8,128)(4,1)}, u32[]{:S(2)}) copy-start(pred[256,256]{0,1:T(8,128)(4,1)} %fusion.28) | copy-start | bytes 196612
  40.1 64.8 %all-to-all-start.1 = ((bf16[8,256,512]{1,2,0:T(8,128)(2,1)}), bf16[8,256,512]{1,2,0:T(8,128)(2,1)}, u32[]{:S(2)}, u32[]{:S(2)}) async-start(bf16[8,256,512]{1,2,0:T(8,128)(2,1)} %broadcast_select_fusion), calls=%async_computation.1 | async-start | bytes 4194304 | tf_op jit(solution)/shard_map/all_to_all | solution.py:123
  46.3 117.9 %reduce-scatter.2.cloned.1.call-start = ((), (), s32[]{:S(2)}) async-start(), calls=%async_computation.5 | async-start | bytes 1310720 | tf_op jit(solution)/shard_map/reduce_scatter | solution.py:158
  55.3 4.9 %copy-start.6 = (bf16[256,256]{1,0:T(8,128)(2,1)}, bf16[256,256]{1,0:T(8,128)(2,1)S(1)}, u32[]{:S(2)}) copy-start(bf16[256,256]{1,0:T(8,128)(2,1)S(1)} %convolution_convert_fusion.1) | copy-start | bytes 393220
  58.9 2.8 %copy-start.1 = (bf16[256,2048]{1,0:T(8,128)(2,1)S(1)}, bf16[256,2048]{1,0:T(8,128)(2,1)}, u32[]{:S(2)}) copy-start(bf16[256,2048]{1,0:T(8,128)(2,1)} %all-gather.5.cloned.1.call-done) | copy-start | bytes 3145732
  58.9 2.8 %copy-start.4 = (bf16[2048,256]{1,0:T(8,128)(2,1)S(1)}, bf16[2048,256]{1,0:T(8,128)(2,1)}, u32[]{:S(2)}) copy-start(bf16[2048,256]{1,0:T(8,128)(2,1)} %param.21) | copy-start | bytes 3145732
  62.8 46.5 %copy-start.8 = (bf16[256,2,128]{2,0,1:T(8,128)(2,1)}, bf16[256,2,128]{2,0,1:T(8,128)(2,1)S(1)}, u32[]{:S(2)}) copy-start(bf16[256,2,128]{2,0,1:T(8,128)(2,1)S(1)} %maximum_convert_fusion) | copy-start | bytes 393220
  106.8 2.5 %copy-start.11 = (bf16[512,2,128]{2,0,1:T(8,128)(2,1)S(1)}, bf16[512,2,128]{2,0,1:T(8,128)(2,1)}, u32[]{:S(2)}) copy-start(bf16[512,2,128]{2,0,1:T(8,128)(2,1)} %copy.128) | copy-start | bytes 786436
  119.3 9.1 %copy-start.2 = (bf16[2048,256]{0,1:T(8,128)(2,1)S(1)}, bf16[2048,256]{0,1:T(8,128)(2,1)}, u32[]{:S(2)}) copy-start(bf16[2048,256]{0,1:T(8,128)(2,1)} %get-tuple-element.27) | copy-start | bytes 3145732
  119.3 9.1 %copy-start.5 = (bf16[512,256]{0,1:T(8,128)(2,1)S(1)}, bf16[512,256]{0,1:T(8,128)(2,1)}, u32[]{:S(2)}) copy-start(bf16[512,256]{0,1:T(8,128)(2,1)} %copy.134) | copy-start | bytes 786436
  119.3 9.1 %copy-start.7 = (bf16[256,256]{0,1:T(8,128)(2,1)S(1)}, bf16[256,256]{0,1:T(8,128)(2,1)}, u32[]{:S(2)}) copy-start(bf16[256,256]{0,1:T(8,128)(2,1)} %copy.135) | copy-start | bytes 393220
  128.4 1.4 copy-start.3
  137.5 1.8 %copy-start.9 = (bf16[256,2,128]{2,0,1:T(8,128)(2,1)S(1)}, bf16[256,2,128]{2,0,1:T(8,128)(2,1)}, u32[]{:S(2)}) copy-start(bf16[256,2,128]{2,0,1:T(8,128)(2,1)} %copy-done.8) | copy-start | bytes 393220
Sparse Core Ops, SparseCore 0:
  11.2 19.4 all-gather.4
  32.7 66.3 all-gather.2
  139.4 24.7 reduce-scatter.1
